TPU v7x, 256 devices: a whole 4x4x8 slice. The times are simulated.
256 devices in a mesh: seq: 32 (over y, z), head: 8 (over x, core).
Axes of the slice: x: 4, y: 4, z: 8, core: 2. Of those that a mesh axis runs over, the one named last changes fastest.
Arguments:
- queries: bfloat16 [16384, 8192], P('seq', 'head'), may hold values from -6 to 6
- keys: bfloat16 [16384, 8192], P('seq', 'head'), may hold values from -6 to 6
- values: bfloat16 [16384, 8192], P('seq', 'head'), may hold values from -6 to 6
- log_decay: float32 [16384, 64], P('seq', 'head'), may hold values from -1.55 to 0, as said below
- gate: bfloat16 [16384, 8192], P('seq', 'head'), may hold values from -6 to 6
- norm_gain: float32 [8192], P('head'), may hold values from 0.1 to 1.9
- w_out: bfloat16 [8192, 3072], P('head'), may hold values from -0.09375 to 0.09375
Outputs:
- output: bfloat16 [16384, 3072], P('seq', 'head')
Inputs may be any that keep to these rules, and one draw needn't show every extreme that they name: log_decay is negative.
All inputs are finite; a program needn't handle non-finite values.
Results may differ from a plain program's by a relative error of at most 0.024.
Values may be sent and summed in bfloat16 or wider, within the bound.
A program may use at most 128 MiB of HBM per device.

v0:
```python
import jax
import jax.numpy as jnp
from jax import lax
from jax.sharding import PartitionSpec as P

HD = 128
BLOCK = 256


def entering_2(array, axis, join, neutral):
    place = lax.axis_index(axis)
    gathered = jax.tree.map(
        lambda a, kind: lax.all_gather(a.astype(kind), axis), array, (jnp.bfloat16, jnp.bfloat16)
    )
    state = jax.tree.map(lambda a, e: jnp.zeros_like(a) + jnp.asarray(e, a.dtype), array, neutral)

    def one(turn, state):
        return join(
            state,
            jax.tree.map(
                lambda a, own: lax.dynamic_index_in_dim(a, turn, 0, False).astype(own.dtype),
                gathered,
                array,
            ),
        )

    return lax.fori_loop(0, place, one, state)


def combine(earlier, later):
    return (earlier[0] + later[0], jnp.exp(later[0])[:, None, None] * earlier[1] + later[1])


def per_device(queries, keys, values, log_decay, gate, norm_gain, w_out):
    row_count, feat_count = queries.shape
    head_count = feat_count // HD
    block_count = row_count // BLOCK
    block_shape = (block_count, BLOCK, head_count, HD)
    query_blocks = queries.reshape(block_shape)
    key_blocks = keys.reshape(block_shape)
    value_blocks = values.reshape(block_shape)
    cumulative = jnp.cumsum(log_decay.reshape(block_count, BLOCK, head_count), axis=1)
    block_total = cumulative[:, -1, :]
    weighted_keys = (
        key_blocks.astype(jnp.float32) * jnp.exp(block_total[:, None, :] - cumulative)[..., None]
    ).astype(jnp.bfloat16)
    block_states = jnp.einsum(
        "bthd,bthe->bhde", weighted_keys, value_blocks, preferred_element_type=jnp.float32
    )

    def local_step(carry_state, block_item):
        block_kv, block_decay = block_item
        return (jnp.exp(block_decay)[:, None, None] * carry_state + block_kv, carry_state)

    empty_state = jnp.zeros((head_count, HD, HD), jnp.float32)
    end_state, local_enter = lax.scan(local_step, empty_state, (block_states, block_total))
    device_total = jnp.sum(block_total, axis=0)
    identity = (jnp.zeros((head_count,), jnp.float32), empty_state)
    prefix_log, prefix_state = entering_2((device_total, end_state), "seq", combine, identity)
    before_block = jnp.cumsum(block_total, axis=0) - block_total
    entering = jnp.exp(before_block)[:, :, None, None] * prefix_state[None] + local_enter
    state_half = entering.astype(jnp.bfloat16)
    query_scaled = (query_blocks.astype(jnp.float32) * jnp.exp(cumulative)[..., None]).astype(
        jnp.bfloat16
    )
    inter_part = jnp.einsum(
        "bihd,bhde->bihe", query_scaled, state_half, preferred_element_type=jnp.float32
    )
    scores = jnp.einsum(
        "bihd,bjhd->bhij", query_blocks, key_blocks, preferred_element_type=jnp.float32
    )
    cum_heads = jnp.swapaxes(cumulative, 1, 2)
    between = cum_heads[..., :, None] - cum_heads[..., None, :]
    causal = jnp.tril(jnp.ones((BLOCK, BLOCK), dtype=bool))
    weights = jnp.where(causal[None, None], jnp.exp(jnp.minimum(between, 0.0)), 0.0)
    scores_half = (scores * weights).astype(jnp.bfloat16)
    intra_part = jnp.einsum(
        "bhij,bjhe->bihe", scores_half, value_blocks, preferred_element_type=jnp.float32
    )
    attended = intra_part + inter_part
    normed = (
        attended
        * lax.rsqrt(jnp.mean(attended * attended, axis=-1, keepdims=True) + 1e-06)
        * norm_gain.reshape(head_count, HD)
    )
    hidden = (
        normed.reshape(row_count, feat_count) * jax.nn.sigmoid(gate.astype(jnp.float32))
    ).astype(jnp.bfloat16)
    partial_value = jnp.dot(hidden, w_out, preferred_element_type=jnp.float32)
    return lax.psum_scatter(
        partial_value.astype(jnp.bfloat16), "head", scatter_dimension=1, tiled=True
    )


def solution(mesh):
    placed = (
        P("seq", "head"),
        P("seq", "head"),
        P("seq", "head"),
        P("seq", "head"),
        P("seq", "head"),
        P("head"),
        P("head", None),
    )
    return jax.shard_map(
        per_device, mesh=mesh, in_specs=placed, out_specs=P("seq", "head"), check_vma=False
    )
```

profile of v0, /device:TPU:24, one launch (start us, length us, event | category | flops | bytes accessed | tf_op | source)
XLA Modules:
  0.0 213.5 jit_solution(3561791059964491350)
XLA Ops:
  6.5 0.0 all-gather.4.cloned.1.call-start
  6.5 2.2 %reduce-window.6 = f32[2,8,2,128]{3,1,2,0:T(8,128)S(1)} reduce-window(f32[2,8,2,128]{3,1,2,0:T(8,128)} %bitcast.71, f32[]{:T(128)} %constant.36.clone.1), window={size=1x1x1x128 pad=0_0x0_0x0_0x127_0}, to_apply=%region_0.0 | reduce-window | flops 520192 | bytes 32772 | tf_op jit(solution)/shard_map/reduce-window
  8.7 0.2 slice_reduce_fusion
  9.0 0.1 fusion.18
  9.0 0.2 slice_reduce_fusion.1
  9.2 0.1 subtract_exponential_fusion
  9.3 1.5 copy.43
  10.8 0.7 copy.34
  11.5 2.6 %copy.44 = bf16[64,8,8,128]{3,2,1,0:T(8,128)(2,1)} copy(bf16[64,8,8,128]{3,1,2,0:T(8,128)(2,1)} %bitcast.67) | data formatting | bytes 2097152
  14.1 1.7 fusion.4
  15.8 0.0 copy-start.3
  15.8 2.0 while.26
  15.8 0.8 bitcast_dynamic-update-slice_fusion.2
  16.6 0.1 bitcast_add_fusion.3
  16.8 0.8 bitcast_dynamic-update-slice_fusion.2
  17.6 0.1 bitcast_add_fusion.3
  17.8 0.0 copy-start
  17.8 0.7 convert_element_type.64
  18.5 0.0 all-gather.4.cloned.1.call-update
  18.6 0.0 reduce-scatter.4.cloned.1.call-start
  18.6 0.0 copy-done.3
  18.6 0.6 dynamic-slice
  19.9 0.2 dynamic-update-slice
  20.1 66.5 %all-reduce = bf16[256]{0:T(256)(128)(2,1)S(1)} all-reduce(bf16[256]{0:T(256)(128)(2,1)S(1)} %dynamic-update-slice), channel_id=2, replica_groups=mesh['seq'=32,'head'=8] {'seq'}, use_global_device_ids=true, to_apply=%add | all-reduce | flops 256 | bytes 1024
  86.6 0.1 reshape.110
  86.7 2.5 %copy.42 = bf16[64,8,8,128]{3,2,1,0:T(8,128)(2,1)} copy(bf16[64,8,8,128]{3,1,2,0:T(8,128)(2,1)} %bitcast.68) | data formatting | bytes 2097152
  89.2 0.1 add_bitcast_fusion.1
  89.3 0.0 copy-done
  89.3 4.3 %fusion.3 = f32[2,8,256,128]{2,3,1,0:T(8,128)} fusion(bf16[2,256,8,128]{1,3,2,0:T(8,128)(2,1)S(1)} %copy.34, f32[2,8,256]{2,1,0:T(8,128)S(1)} %add_bitcast_fusion.1, pred[256,256]{1,0:T(8,128)(4,1)S(1)} %iota_compare_fusion, bf16[2,256,8,128]{3,2,1,0:T(8,128)(2,1)S(1)} %bitcast.61, bf16[2,256,8,128]{3,2,1,0:T(8,128)(2,1)} %bitcast.63), kind=kOutput, calls=%fused_computation.16 | convolution fusion | flops 542113792 | bytes 5324800 | tf_op jit(solution)/shard_map/bhij,bjhe->bihe/dot_general | solution.py:77
  93.6 24.5 %all-gather.4.cloned.1.call-done = bf16[256,128,128]{2,1,0:T(8,128)(2,1)} async-done(((bf16[8,128,128]{2,1,0:T(8,128)(2,1)}), bf16[256,128,128]{2,1,0:T(8,128)(2,1)}) %all-gather.4.cloned.1.call-update) | async-done | bytes 8388624 | tf_op jit(solution)/shard_map/all_gather | solution.py:13
  118.2 27.8 %while.25 = (s32[]{:T(128)}, f32[8,128,128]{2,1,0:T(8,128)S(1)}, s32[]{:T(128)}, bf16[32,8]{1,0:T(8,128)(2,1)S(1)}, bf16[32,8,128,128]{3,2,1,0:T(8,128)(2,1)}, /*index=5*/s32[]{:T(128)}, s32[]{:T(128)}, s32[]{:T(128)}) while((s32[]{:T(128)}, f32[8,128,128]{2,1,0:T(8,128)S(1)}, s32[]{:T(128)}, bf16[32,8]{1,0:T(8,128)(2,1)S(1)}, ...), condition=%wide.region_7.8_spmd, body=%wide.region_6.7_spmd.sunk | while | flops 393229 | bytes 1310927 | solution.py:27
  118.2 1.2 convert_add_fusion.2
  119.4 1.1 convert_add_fusion.2
  120.6 1.1 convert_add_fusion.2
  121.7 1.1 convert_add_fusion.2
  122.9 1.1 convert_add_fusion.2
  124.1 1.1 convert_add_fusion.2
  125.2 1.1 convert_add_fusion.2
  126.4 1.1 convert_add_fusion.2
  127.5 1.1 convert_add_fusion.2
  128.7 1.1 convert_add_fusion.2
  129.8 1.1 convert_add_fusion.2
  131.0 1.1 convert_add_fusion.2
  132.1 1.1 convert_add_fusion.2
  133.3 1.1 convert_add_fusion.2
  134.5 1.1 convert_add_fusion.2
  135.6 1.1 convert_add_fusion.2
  136.8 1.1 convert_add_fusion.2
  137.9 1.1 convert_add_fusion.2
  139.1 1.1 convert_add_fusion.2
  140.2 1.1 convert_add_fusion.2
  141.4 1.1 convert_add_fusion.2
  142.5 1.1 convert_add_fusion.2
  143.7 1.1 convert_add_fusion.2
  144.9 1.1 convert_add_fusion.2
  146.0 0.0 copy-start.2
  146.0 3.2 %multiply_reduce_fusion = (f32[2,256,8]{1,2,0:T(8,128)S(1)}, f32[2,256,8,128]{1,3,2,0:T(8,128)S(1)}) fusion(f32[2,256,8]{1,2,0:T(8,128)S(1)} %get-tuple-element.120, bf16[2,256,8,128]{3,2,1,0:T(8,128)(2,1)S(1)} %bitcast.64, f32[2,8,128,128]{3,2,1,0:T(8,128)} %get-tuple-element.79, f32[8,128,128]{2,1,0:T(8,128)S(1)} %get-tuple-element.78, ...), kind=kOutput, calls=%fused_computation.13 | convolution fusion | flops 138145792 | bytes 6848576 | tf_op jit(solution)/shard_map/bihd,bhde->bihe/dot_general | solution.py:66
  149.3 0.3 multiply_multiply_fusion
  149.6 1.9 copy.38
  151.5 7.2 %convolution_convert_fusion = bf16[512,3072]{1,0:T(8,128)(2,1)S(1)} fusion(bf16[1024,3072]{1,0:T(8,128)(2,1)} %param.17, f32[64,8,8,128]{3,2,1,0:T(8,128)} %bitcast.65, bf16[512,1024]{1,0:T(8,128)(2,1)} %param.15), kind=kOutput, calls=%fused_computation.7 | convolution fusion | flops 3225944064 | bytes 12582912 | tf_op jit(solution)/shard_map/dot_general | solution.py:89
  158.7 2.8 %copy.40 = bf16[512,3072]{0,1:T(8,128)(2,1)} copy(bf16[512,3072]{1,0:T(8,128)(2,1)S(1)} %convolution_convert_fusion) | data formatting | bytes 6291456
  161.5 0.0 reduce-scatter.4.cloned.1.call-update
  161.6 43.2 %reduce-scatter.4.cloned.1.call-done = bf16[384,512]{1,0:T(8,128)(2,1)} async-done(((bf16[3072,512]{1,0:T(8,128)(2,1)}), bf16[384,512]{1,0:T(8,128)(2,1)}) %reduce-scatter.4.cloned.1.call-update) | async-done | bytes 393232
  204.7 1.9 copy.41
  (39 shorter events, 0.5 us)
Async XLA Ops:
  6.5 111.6 %all-gather.4.cloned.1.call-start = ((), (), s32[]{:S(2)}) async-start(), calls=%async_computation.1 | async-start | bytes 8650752 | tf_op jit(solution)/shard_map/all_gather | solution.py:13
  15.8 2.9 %copy-start.3 = (u32[256]{0:T(256)S(1)}, u32[256]{0:T(256)}, u32[]{:S(2)}) copy-start(u32[256]{0:T(256)} %constant.58) | copy-start | bytes 3076
  17.8 71.5 %copy-start = (bf16[64,8,8,128]{3,2,1,0:T(8,128)(2,1)S(1)}, bf16[64,8,8,128]{3,2,1,0:T(8,128)(2,1)}, u32[]{:S(2)}) copy-start(bf16[64,8,8,128]{3,2,1,0:T(8,128)(2,1)} %copy.44) | copy-start | bytes 3145732
  18.6 186.2 %reduce-scatter.4.cloned.1.call-start = ((), (), s32[]{:S(2)}) async-start(), calls=%async_computation.2 | async-start | bytes 3538944
  118.1 27.8 %copy-start.1 = (bf16[64,8,8,128]{3,2,1,0:T(8,128)(2,1)S(1)}, bf16[64,8,8,128]{3,2,1,0:T(8,128)(2,1)}, u32[]{:S(2)}) copy-start(bf16[64,8,8,128]{3,2,1,0:T(8,128)(2,1)} %copy.42) | copy-start | bytes 3145732
  146.0 3.3 %copy-start.2 = (f32[1024]{0:T(1024)S(1)}, f32[1024]{0:T(1024)}, u32[]{:S(2)}) copy-start(f32[1024]{0:T(1024)} %param.16) | copy-start | bytes 12292
Sparse Core Ops, SparseCore 0:
  18.7 99.3 all-gather.3
  161.7 42.9 reduce-scatter.3
where the time goes:
time: 215 us; the launch traced here: 213 us
  waiting for transfers between devices  67.7 us (31%)
  blocking collectives  66.5 us (31%)
  other arithmetic  32.7 us (15%)
  matrix products  16.5 us (8%)
  local copies, waits for them, and re-layouts  15.1 us (7%)
  between operations  14.2 us (7%)
    unnamed x1, blocking collectives  66.5 us
    unnamed x3, waiting for transfers between devices  43.2 us
    add x24, other arithmetic, combine(): jnp.exp(later[0])[:, None, None] * earlier[1] + later[1]  26.7 us
    all_gather x1, waiting for transfers between devices, entering_2(): lax.all_gather(a.astype(kind), axis)  24.5 us
    unnamed x16, local copies, waits for them, and re-layouts  12.2 us
    dot_general x1, matrix products, per_device(): partial_value = jnp.dot(hidden, w_out, preferred_element_type=jnp.float32)  7.24 us
    dot_general x1, matrix products, per_device(): jnp.einsum('bhij,bjhe->bihe', scores_half, value_blocks, preferred_elemen...  4.32 us
  transfers between devices with their start and end apart: 2, of which 2 were waited for; matrix products, arithmetic and copies ran while one was open for 4% of the time, Pallas kernels for 0%

commit v1 on v0

v1 whole, which is shorter than its diff:
```python
import jax
import jax.numpy as jnp
from jax import lax
from jax.experimental import pallas as pl
from jax.experimental.pallas import tpu as pltpu
from jax.sharding import PartitionSpec as P

HD = 128
BLOCK = 256
NX, NY, NZ = 4, 4, 8
ROWS = 512
HEADS = 8
FEAT = HEADS * HD
CW = 384
TILE = 128
NT = ROWS // TILE
HALF = TILE // 2
EARLY = 4

F32, BF16 = jnp.float32, jnp.bfloat16
EXACT = lax.Precision.HIGHEST
MESH = pl.DeviceIdType.MESH


def remote(src, dst, send_sem, recv_sem, device_id):
    return pltpu.make_async_remote_copy(
        src_ref=src,
        dst_ref=dst,
        send_sem=send_sem,
        recv_sem=recv_sem,
        device_id=device_id,
        device_id_type=MESH,
    )


def columns(index, width=HD):
    return pl.ds(pl.multiple_of(index * width, HD), width)


def kernel(
    q_hbm, k_hbm, v_hbm, ld_hbm, gate_hbm, gain_hbm, w_hbm,
    out,
    q, k, v, ld, gate, gain, w_own, w_peer,
    cb, cumr, att, qs, gg, h_own, h_peer,
    lt, ltb, s_end, s_first, s_in, w_pre, cl_pre, t_out, t_in, rd_out, rd_in, p_out, p_in,
    opp, side, held, fwd, mine, passing, fin,
    load_sem, lt_s, lt_r, s1, r1, t_s, t_r, rd_s, rd_r, s3, r3, w_s, w_r, h_s, h_r,
    m1_s, m1_r, m2_s, m2_r, m3_s, m3_r,
):
    head, seq = lax.axis_index("head"), lax.axis_index("seq")
    z, y = lax.rem(seq, NZ), lax.div(seq, NZ)
    row0 = seq - z
    core, x = lax.rem(head, 2), lax.div(head, 2)
    other = {"head": head + 1 - 2 * core}
    x_right, x_left, x_opp = lax.rem(x + 1, NX), lax.rem(x + 3, NX), lax.rem(x + 2, NX)
    right, left = {"head": x_right * 2 + core}, {"head": x_left * 2 + core}

    def along_z(off):
        return lax.rem(z + off, NZ)

    def along_y(off):
        return lax.rem(y + off, NY)

    loads = [
        pltpu.make_async_copy(src, dst, load_sem.at[i])
        for i, (src, dst) in enumerate(
            ((ld_hbm, ld), (k_hbm, k), (v_hbm, v), (q_hbm, q), (gate_hbm, gate), (gain_hbm, gain))
        )
    ]
    w_loads = [
        pltpu.make_async_copy(
            w_hbm.at[:, pl.ds(pl.multiple_of((2 * i + core) * CW, HD), CW)],
            w_own.at[i],
            load_sem.at[6 + i],
        )
        for i in range(NX)
    ]
    w_sends = [
        remote(
            w_hbm.at[:, pl.ds(pl.multiple_of((2 * i + 1 - core) * CW, HD), CW)],
            w_peer.at[i],
            w_s.at[i],
            w_r.at[i],
            other,
        )
        for i in range(NX)
    ]
    for copy in loads:
        copy.start()

    barrier = pltpu.get_barrier_semaphore()
    for off in range(1, NZ):
        pl.semaphore_signal(
            barrier, inc=1, device_id={"seq": row0 + along_z(off)}, device_id_type=MESH
        )
    for off in range(1, NY):
        pl.semaphore_signal(
            barrier, inc=1, device_id={"seq": along_y(off) * NZ + z}, device_id_type=MESH
        )
    for device in (other, right, left):
        pl.semaphore_signal(barrier, inc=1, device_id=device, device_id_type=MESH)

    at_row = lax.broadcasted_iota(jnp.int32, (BLOCK, BLOCK), 0)
    at_col = lax.broadcasted_iota(jnp.int32, (BLOCK, BLOCK), 1)
    lower = jnp.where(at_row >= at_col, 1.0, 0.0).astype(F32)
    upper = jnp.where(at_row <= at_col, 1.0, 0.0).astype(F32)
    loads[0].wait()
    for b in range(2):
        rows = slice(b * BLOCK, (b + 1) * BLOCK)
        decay = ld[rows, :]
        cum = jnp.dot(lower, decay, precision=EXACT, preferred_element_type=F32)
        cumr[:, rows] = lax.dot_general(
            decay, upper, (((0,), (0,)), ((), ())), precision=EXACT, preferred_element_type=F32
        )
        for h in range(HEADS):
            cb[rows, h * HD : (h + 1) * HD] = jnp.broadcast_to(cum[:, h : h + 1], (BLOCK, HD))
    lt[...] = jnp.broadcast_to(
        cumr[:, BLOCK - 1 : BLOCK] + cumr[:, ROWS - 1 : ROWS], (HEADS, HD)
    )
    ltb[z] = lt[...]
    pl.semaphore_wait(barrier, NZ - 1 + NY - 1 + 3)

    def lt_copy(off):
        return remote(
            lt, ltb.at[z], lt_s.at[off], lt_r.at[z], {"seq": row0 + along_z(off)}
        )

    for off in range(1, NZ):
        lt_copy(off).start()

    def state_copy(h):
        return remote(s_end.at[h], s_in.at[z], s1.at[h], r1.at[z], {"seq": row0 + h})

    loads[1].wait()
    loads[2].wait()

    @pl.loop(0, HEADS)
    def _(i):
        odd = lax.rem(i, 2)
        h = along_z(4 + lax.div(i + 1, 2) * (2 * odd - 1))
        hc = columns(h)
        parts = []
        for b in range(2):
            rows = slice(b * BLOCK, (b + 1) * BLOCK)
            total = cb[(b + 1) * BLOCK - 1 : (b + 1) * BLOCK, hc]
            weighted = (k[rows, hc].astype(F32) * jnp.exp(total - cb[rows, hc])).astype(BF16)
            parts.append(
                lax.dot_general(
                    weighted, v[rows, hc], (((0,), (0,)), ((), ())), preferred_element_type=F32
                )
            )
        s_first[h] = parts[0].astype(BF16)
        whole = (jnp.exp(cb[ROWS - 1 : ROWS, hc]) * parts[0] + parts[1]).astype(BF16)
        s_end[h] = whole

        @pl.when(i < HEADS - 1)
        def _():
            state_copy(h).start()

        @pl.when(i == HEADS - 1)
        def _():
            s_in[z] = whole

    for copy in w_sends:
        copy.start()
    for copy in w_loads:
        copy.start()
    for copy in loads[3:]:
        copy.wait()

    def within(h):
        hc = columns(h)
        for b in range(2):
            rows = slice(b * BLOCK, (b + 1) * BLOCK)
            query = q[rows, hc]
            scores = lax.dot_general(
                query, k[rows, hc], (((1,), (1,)), ((), ())), preferred_element_type=F32
            )
            col = cb[rows, hc]
            between = jnp.concatenate([col, col], axis=1) - cumr[pl.ds(h, 1), rows]
            weights = jnp.exp(jnp.where(at_row >= at_col, jnp.minimum(between, 0.0), -1e30))
            attended = jnp.dot(
                (scores * weights).astype(BF16), v[rows, hc], preferred_element_type=F32
            )
            scaled = query.astype(F32) * jnp.exp(col)
            if b == 1:
                attended += jnp.dot(
                    scaled.astype(BF16), s_first[h], preferred_element_type=F32
                )
                scaled = query.astype(F32) * jnp.exp(col + cb[BLOCK - 1 : BLOCK, hc])
            qs[rows, hc] = scaled.astype(BF16)
            att[rows, hc] = attended
            gg[rows, hc] = gain[pl.ds(h, 1), :] * jax.nn.sigmoid(gate[rows, hc].astype(F32))

    @pl.loop(0, EARLY)
    def _(h):
        within(h)

    for off in range(1, NZ):
        there = along_z(off)
        remote(lt, ltb.at[there], lt_s.at[off], lt_r.at[there], other).wait_recv()
        remote(s_end.at[0], s_in.at[there], s1.at[0], r1.at[there], other).wait_recv()
    state = jnp.zeros((HD, HD), F32)
    log = jnp.zeros((1, HD), F32)
    for there in range(NZ):
        w_pre[there] = state
        cl_pre[there : there + 1, :] = log
        step = ltb[there, pl.ds(z, 1), :]
        state = jnp.exp(step) * state + s_in[there].astype(F32)
        log = log + step
    t_out[...] = state.astype(BF16)
    rd_out[...] = jnp.broadcast_to(log, (8, HD))
    t_in[y] = t_out[...]
    rd_in[y] = rd_out[...]

    def row_copies(off):
        device = {"seq": along_y(off) * NZ + z}
        return (
            remote(t_out, t_in.at[y], t_s.at[off], t_r.at[y], device),
            remote(rd_out, rd_in.at[y], rd_s.at[off], rd_r.at[y], device),
        )

    for off in range(1, NY):
        for copy in row_copies(off):
            copy.start()
    for off in range(1, NY):
        there = along_y(off)
        remote(t_out, t_in.at[there], t_s.at[off], t_r.at[there], other).wait_recv()
        remote(rd_out, rd_in.at[there], rd_s.at[off], rd_r.at[there], other).wait_recv()
    before = jnp.zeros((HD, HD), F32)
    for there in range(NY - 1):
        joined = jnp.exp(rd_in[there][0:1, :]) * before + t_in[there].astype(F32)
        before = jnp.where(there < y, joined, before)

    def prefix_copy(there):
        return remote(
            p_out.at[there], p_in.at[z], s3.at[there], r3.at[z], {"seq": row0 + there}
        )

    for off in (4, 5, 3, 6, 2, 7, 1, 0):
        there = along_z(off)
        entering = (
            jnp.exp(cl_pre[pl.ds(there, 1), :]) * before + w_pre[there]
        ).astype(BF16)
        if off:
            p_out[there] = entering
            prefix_copy(there).start()
        else:
            p_in[z] = entering

    @pl.loop(EARLY, HEADS)
    def _(h):
        within(h)

    for copy in w_loads:
        copy.wait()
    for copy in w_sends:
        copy.wait_recv()
    for off in range(1, NZ):
        there = along_z(off)
        remote(p_out.at[0], p_in.at[there], s3.at[0], r3.at[there], other).wait_recv()

    def tile(t):
        return pl.ds(pl.multiple_of(t * TILE, TILE), TILE)

    def hidden_copy(t):
        return remote(h_own.at[tile(t)], h_peer.at[tile(t)], h_s.at[t], h_r.at[t], other)

    def make_hidden(t):
        rows = tile(t)
        for h in range(HEADS):
            hc = slice(h * HD, (h + 1) * HD)
            attended = att[rows, hc] + jnp.dot(
                qs[rows, hc], p_in[h], preferred_element_type=F32
            )
            square = jnp.mean(attended * attended, axis=1, keepdims=True)
            h_own[rows, hc] = (attended * lax.rsqrt(square + 1e-06) * gg[rows, hc]).astype(BF16)
        hidden_copy(t).start()

    def chunk(t, i):
        return jnp.dot(h_own[tile(t), :], w_own[i], preferred_element_type=F32) + jnp.dot(
            h_peer[tile(t), :], w_peer[i], preferred_element_type=F32
        )

    targets = (right, left)
    halves = (slice(0, HALF), slice(HALF, TILE))

    def first_copy(t, way):
        return remote(
            opp.at[t, way], fwd.at[way, t], m1_s.at[way, t], m1_r.at[way, t], targets[way]
        )

    def side_copy(t, way):
        return remote(
            side.at[way, t], fin.at[way, t, 1 - way], m2_s.at[way, t], m2_r.at[way, t], targets[way]
        )

    def passing_copy(t, way):
        return remote(
            passing.at[way, t], fin.at[way, t, way], m3_s.at[way, t], m3_r.at[way, t], targets[way]
        )

    def project(t):
        hidden_copy(t).wait_recv()
        far = chunk(t, x_opp).astype(BF16)
        for way in range(2):
            opp[t, way] = far[halves[way]]
            first_copy(t, way).start()
        for way, i in enumerate((x_right, x_left)):
            near = chunk(t, i)
            side[way, t] = near[halves[1 - way]].astype(BF16)
            side_copy(t, way).start()
            held[way, t] = near[halves[way]]
        mine[t] = chunk(t, x)

    def pass_on(t):
        for way in range(2):
            first_copy(t, way).wait_recv()
            passing[way, t] = (held[way, t] + fwd[way, t].astype(F32)).astype(BF16)
            passing_copy(t, way).start()

    make_hidden(0)

    @pl.loop(0, NT)
    def _(t):
        @pl.when(t < NT - 1)
        def _():
            make_hidden(t + 1)

        project(t)

        @pl.when(t > 0)
        def _():
            pass_on(t - 1)

    pass_on(NT - 1)

    @pl.loop(0, NT)
    def _(t):
        for way in range(2):
            side_copy(t, way).wait_recv()
            passing_copy(t, way).wait_recv()
        for half in range(2):
            rows = pl.ds(pl.multiple_of(t * TILE + half * HALF, HALF), HALF)
            out[rows, :] = (
                mine[t, halves[half]]
                + fin[0, t, half].astype(F32)
                + fin[1, t, half].astype(F32)
            ).astype(BF16)

    for off in range(1, NZ):
        lt_copy(off).wait_send()
        there = along_z(off)
        state_copy(there).wait_send()
        prefix_copy(there).wait_send()
    for off in range(1, NY):
        for copy in row_copies(off):
            copy.wait_send()
    for copy in w_sends:
        copy.wait_send()

    @pl.loop(0, NT)
    def _(t):
        hidden_copy(t).wait_send()
        for way in range(2):
            first_copy(t, way).wait_send()
            side_copy(t, way).wait_send()
            passing_copy(t, way).wait_send()


def per_device(queries, keys, values, log_decay, gate, norm_gain, w_out):
    vmem, dma = pltpu.VMEM, pltpu.SemaphoreType.DMA
    scratch = [
        vmem((ROWS, FEAT), BF16),
        vmem((ROWS, FEAT), BF16),
        vmem((ROWS, FEAT), BF16),
        vmem((ROWS, HEADS), F32),
        vmem((ROWS, FEAT), BF16),
        vmem((HEADS, HD), F32),
        vmem((NX, FEAT, CW), BF16),
        vmem((NX, FEAT, CW), BF16),
        vmem((ROWS, FEAT), F32),
        vmem((HEADS, ROWS), F32),
        vmem((ROWS, FEAT), F32),
        vmem((ROWS, FEAT), BF16),
        vmem((ROWS, FEAT), F32),
        vmem((ROWS, FEAT), BF16),
        vmem((ROWS, FEAT), BF16),
        vmem((HEADS, HD), F32),
        vmem((NZ, HEADS, HD), F32),
        vmem((HEADS, HD, HD), BF16),
        vmem((HEADS, HD, HD), BF16),
        vmem((NZ, HD, HD), BF16),
        vmem((NZ, HD, HD), F32),
        vmem((NZ, HD), F32),
        vmem((HD, HD), BF16),
        vmem((NY, HD, HD), BF16),
        vmem((8, HD), F32),
        vmem((NY, 8, HD), F32),
        vmem((NZ, HD, HD), BF16),
        vmem((HEADS, HD, HD), BF16),
        vmem((NT, 2, HALF, CW), BF16),
        vmem((2, NT, HALF, CW), BF16),
        vmem((2, NT, HALF, CW), F32),
        vmem((2, NT, HALF, CW), BF16),
        vmem((NT, TILE, CW), F32),
        vmem((2, NT, HALF, CW), BF16),
        vmem((2, NT, 2, HALF, CW), BF16),
        dma((6 + NX,)),
        dma((NZ,)), dma((NZ,)),
        dma((NZ,)), dma((NZ,)),
        dma((NY,)), dma((NY,)),
        dma((NY,)), dma((NY,)),
        dma((NZ,)), dma((NZ,)),
        dma((NX,)), dma((NX,)),
        dma((NT,)), dma((NT,)),
        dma((2, NT)), dma((2, NT)),
        dma((2, NT)), dma((2, NT)),
        dma((2, NT)), dma((2, NT)),
    ]
    return pl.pallas_call(
        kernel,
        out_shape=jax.ShapeDtypeStruct((ROWS, CW), BF16),
        in_specs=[pl.BlockSpec(memory_space=pl.ANY)] * 7,
        out_specs=pl.BlockSpec(memory_space=pltpu.VMEM),
        scratch_shapes=scratch,
        compiler_params=pltpu.CompilerParams(
            collective_id=0, has_side_effects=True, vmem_limit_bytes=56 * 1024 * 1024
        ),
        cost_estimate=pl.CostEstimate(
            flops=2 * ROWS * FEAT * (3072 + 2 * BLOCK + 2 * HD),
            bytes_accessed=11_000_000,
            transcendentals=ROWS * FEAT * 4,
        ),
    )(queries, keys, values, log_decay, gate, norm_gain.reshape(HEADS, HD), w_out)


def solution(mesh):
    placed = (
        P("seq", "head"),
        P("seq", "head"),
        P("seq", "head"),
        P("seq", "head"),
        P("seq", "head"),
        P("head"),
        P("head", None),
    )
    return jax.shard_map(
        per_device, mesh=mesh, in_specs=placed, out_specs=P("seq", "head"), check_vma=False
    )
```

time: 215 us -> 53 us (0.25)
  the two profiles are of different devices: /device:TPU:24 before, /device:TPU:1 now
where the time goes in v1:
time: 53 us; the launch traced here: 52.8 us
  Pallas kernels  49.5 us (93%)
  local copies, waits for them, and re-layouts  3.33 us (6%)
    pallas_call x1, Pallas kernels, per_device(): pl.pallas_call(kernel, out_shape=jax.ShapeDtypeStruct((ROWS, CW), BF16),...  49.5 us
    unnamed x2, local copies, waits for them, and re-layouts  3.33 us

profile of v1, /device:TPU:1, one launch (start us, length us, event | category | flops | bytes accessed | tf_op | source)
XLA Modules:
  0.0 52.8 jit_solution(10430264407594920262)
XLA Ops:
  0.0 1.6 %copy.8.ld_hbm = f32[512,8]{1,0:T(8,128)} copy(f32[512,8]{0,1:T(8,128)} %param.10) | data formatting | bytes 32768 | tf_op args[3]
  1.6 49.5 %shard_map.73 = bf16[512,384]{1,0:T(8,128)(2,1)} custom-call(bf16[512,1024]{1,0:T(8,128)(2,1)} %q_hbm.1, bf16[512,1024]{1,0:T(8,128)(2,1)} %k_hbm.1, bf16[512,1024]{1,0:T(8,128)(2,1)} %v_hbm.1, f32[512,8]{1,0:T(8,128)} %copy.8.ld_hbm, bf16[512,1024]{1,0:T(8,128)(2,1)} %gate_hbm.1, f32[8,128]{1,0:T(8,128)} %bitcast.1, bf16[1024,3072]{1,0:T(8,128)(2,1)} %w_hbm.1), custom_call_target="tpu_custom_call" | custom-call | flops 4026531840 | bytes 11000000 | tf_op jit(solution)/shard_map/pallas_call | solution.py:421
  51.0 1.8 %copy.10 = bf16[512,384]{1,0:T(8,128)(2,1)} copy(bf16[512,384]{1,0:T(8,128)(2,1)} %shard_map.73) | data formatting | bytes 786432

commit v2 on v1

--- a/solution.py
+++ b/solution.py
@@ -15,7 +15,7 @@
 TILE = 128
 NT = ROWS // TILE
 HALF = TILE // 2
-EARLY = 4
+EARLY = 6
 
 F32, BF16 = jnp.float32, jnp.bfloat16
 EXACT = lax.Precision.HIGHEST
@@ -42,7 +42,7 @@
     out,
     q, k, v, ld, gate, gain, w_own, w_peer,
     cb, cumr, att, qs, gg, h_own, h_peer,
-    lt, ltb, s_end, s_first, s_in, w_pre, cl_pre, t_out, t_in, rd_out, rd_in, p_out, p_in,
+    lt, ltb, s_end, s_first, s_in, w_pre, cl_pre, t_out, t_in, rd_out, rd_in, rows_before, p_out, p_in,
     opp, side, held, fwd, mine, passing, fin,
     load_sem, lt_s, lt_r, s1, r1, t_s, t_r, rd_s, rd_r, s3, r3, w_s, w_r, h_s, h_r,
     m1_s, m1_r, m2_s, m2_r, m3_s, m3_r,
@@ -107,37 +107,27 @@
     loads[0].wait()
     for b in range(2):
         rows = slice(b * BLOCK, (b + 1) * BLOCK)
-        decay = ld[rows, :]
-        cum = jnp.dot(lower, decay, precision=EXACT, preferred_element_type=F32)
-        cumr[:, rows] = lax.dot_general(
-            decay, upper, (((0,), (0,)), ((), ())), precision=EXACT, preferred_element_type=F32
-        )
+        decay = ld[:, rows]
+        cum = lax.dot_general(
+            lower, decay, (((1,), (1,)), ((), ())), precision=EXACT, preferred_element_type=F32
+        )
+        cumr[:, rows] = jnp.dot(decay, upper, precision=EXACT, preferred_element_type=F32)
         for h in range(HEADS):
             cb[rows, h * HD : (h + 1) * HD] = jnp.broadcast_to(cum[:, h : h + 1], (BLOCK, HD))
     lt[...] = jnp.broadcast_to(
         cumr[:, BLOCK - 1 : BLOCK] + cumr[:, ROWS - 1 : ROWS], (HEADS, HD)
     )
     ltb[z] = lt[...]
-    pl.semaphore_wait(barrier, NZ - 1 + NY - 1 + 3)
 
     def lt_copy(off):
         return remote(
             lt, ltb.at[z], lt_s.at[off], lt_r.at[z], {"seq": row0 + along_z(off)}
         )
 
-    for off in range(1, NZ):
-        lt_copy(off).start()
-
     def state_copy(h):
         return remote(s_end.at[h], s_in.at[z], s1.at[h], r1.at[z], {"seq": row0 + h})
 
-    loads[1].wait()
-    loads[2].wait()
-
-    @pl.loop(0, HEADS)
-    def _(i):
-        odd = lax.rem(i, 2)
-        h = along_z(4 + lax.div(i + 1, 2) * (2 * odd - 1))
+    def make_state(h):
         hc = columns(h)
         parts = []
         for b in range(2):
@@ -150,17 +140,32 @@
                 )
             )
         s_first[h] = parts[0].astype(BF16)
-        whole = (jnp.exp(cb[ROWS - 1 : ROWS, hc]) * parts[0] + parts[1]).astype(BF16)
-        s_end[h] = whole
-
-        @pl.when(i < HEADS - 1)
-        def _():
-            state_copy(h).start()
-
-        @pl.when(i == HEADS - 1)
-        def _():
-            s_in[z] = whole
-
+        s_end[h] = (jnp.exp(cb[ROWS - 1 : ROWS, hc]) * parts[0] + parts[1]).astype(BF16)
+
+    def far_first(i):
+        return along_z(4 + lax.div(i + 1, 2) * (2 * lax.rem(i, 2) - 1))
+
+    ready = jnp.where(z < NZ // 2, HEADS - 1, 1)
+    loads[1].wait()
+    loads[2].wait()
+
+    @pl.loop(0, HEADS)
+    def _(i):
+        make_state(far_first(i))
+
+        @pl.when(i == ready)
+        def _():
+            pl.semaphore_wait(barrier, NZ - 1 + NY - 1 + 3)
+            for off in range(1, NZ):
+                lt_copy(off).start()
+
+        @pl.when(i >= ready)
+        def _():
+            @pl.loop(jnp.where(i == ready, 0, i), jnp.minimum(i + 1, HEADS - 1))
+            def _(j):
+                state_copy(far_first(j)).start()
+
+    s_in[z] = s_end[z]
     for copy in w_sends:
         copy.start()
     for copy in w_loads:
@@ -196,57 +201,64 @@
     def _(h):
         within(h)
 
-    for off in range(1, NZ):
-        there = along_z(off)
-        remote(lt, ltb.at[there], lt_s.at[off], lt_r.at[there], other).wait_recv()
-        remote(s_end.at[0], s_in.at[there], s1.at[0], r1.at[there], other).wait_recv()
     state = jnp.zeros((HD, HD), F32)
     log = jnp.zeros((1, HD), F32)
     for there in range(NZ):
         w_pre[there] = state
         cl_pre[there : there + 1, :] = log
+
+        @pl.when(there != z)
+        def _():
+            remote(lt, ltb.at[there], lt_s.at[0], lt_r.at[there], other).wait_recv()
+            remote(s_end.at[0], s_in.at[there], s1.at[0], r1.at[there], other).wait_recv()
+
         step = ltb[there, pl.ds(z, 1), :]
         state = jnp.exp(step) * state + s_in[there].astype(F32)
         log = log + step
     t_out[...] = state.astype(BF16)
     rd_out[...] = jnp.broadcast_to(log, (8, HD))
-    t_in[y] = t_out[...]
-    rd_in[y] = rd_out[...]
-
-    def row_copies(off):
-        device = {"seq": along_y(off) * NZ + z}
+
+    def row_copies(there):
+        device = {"seq": there * NZ + z}
         return (
-            remote(t_out, t_in.at[y], t_s.at[off], t_r.at[y], device),
-            remote(rd_out, rd_in.at[y], rd_s.at[off], rd_r.at[y], device),
-        )
-
-    for off in range(1, NY):
-        for copy in row_copies(off):
-            copy.start()
-    for off in range(1, NY):
-        there = along_y(off)
-        remote(t_out, t_in.at[there], t_s.at[off], t_r.at[there], other).wait_recv()
-        remote(rd_out, rd_in.at[there], rd_s.at[off], rd_r.at[there], other).wait_recv()
-    before = jnp.zeros((HD, HD), F32)
+            remote(t_out, t_in.at[y], t_s.at[there], t_r.at[y], device),
+            remote(rd_out, rd_in.at[y], rd_s.at[there], rd_r.at[y], device),
+        )
+
+    for there in range(1, NY):
+
+        @pl.when(there > y)
+        def _():
+            for copy in row_copies(there):
+                copy.start()
+
+    rows_before[...] = jnp.zeros((HD, HD), F32)
     for there in range(NY - 1):
-        joined = jnp.exp(rd_in[there][0:1, :]) * before + t_in[there].astype(F32)
-        before = jnp.where(there < y, joined, before)
+
+        @pl.when(there < y)
+        def _():
+            remote(t_out, t_in.at[there], t_s.at[0], t_r.at[there], other).wait_recv()
+            remote(rd_out, rd_in.at[there], rd_s.at[0], rd_r.at[there], other).wait_recv()
+            rows_before[...] = jnp.exp(rd_in[there][0:1, :]) * rows_before[...] + t_in[
+                there
+            ].astype(F32)
+
+    before = rows_before[...]
 
     def prefix_copy(there):
         return remote(
             p_out.at[there], p_in.at[z], s3.at[there], r3.at[z], {"seq": row0 + there}
         )
 
-    for off in (4, 5, 3, 6, 2, 7, 1, 0):
-        there = along_z(off)
-        entering = (
-            jnp.exp(cl_pre[pl.ds(there, 1), :]) * before + w_pre[there]
-        ).astype(BF16)
-        if off:
-            p_out[there] = entering
+    for there in range(NZ):
+        entering = (jnp.exp(cl_pre[there : there + 1, :]) * before + w_pre[there]).astype(BF16)
+        p_out[there] = entering
+
+        @pl.when(there != z)
+        def _():
             prefix_copy(there).start()
-        else:
-            p_in[z] = entering
+
+    p_in[z] = p_out[z]
 
     @pl.loop(EARLY, HEADS)
     def _(h):
@@ -300,18 +312,19 @@
             passing.at[way, t], fin.at[way, t, way], m3_s.at[way, t], m3_r.at[way, t], targets[way]
         )
 
-    def project(t):
+    def send_far(t):
         hidden_copy(t).wait_recv()
         far = chunk(t, x_opp).astype(BF16)
         for way in range(2):
             opp[t, way] = far[halves[way]]
             first_copy(t, way).start()
+
+    def send_near(t):
         for way, i in enumerate((x_right, x_left)):
             near = chunk(t, i)
             side[way, t] = near[halves[1 - way]].astype(BF16)
             side_copy(t, way).start()
             held[way, t] = near[halves[way]]
-        mine[t] = chunk(t, x)
 
     def pass_on(t):
         for way in range(2):
@@ -327,11 +340,19 @@
         def _():
             make_hidden(t + 1)
 
-        project(t)
+        send_far(t)
+
+    @pl.loop(0, NT)
+    def _(t):
+        send_near(t)
 
         @pl.when(t > 0)
         def _():
             pass_on(t - 1)
+
+    @pl.loop(0, NT)
+    def _(t):
+        mine[t] = chunk(t, x)
 
     pass_on(NT - 1)
 
@@ -353,9 +374,13 @@
         there = along_z(off)
         state_copy(there).wait_send()
         prefix_copy(there).wait_send()
-    for off in range(1, NY):
-        for copy in row_copies(off):
-            copy.wait_send()
+    for there in range(1, NY):
+
+        @pl.when(there > y)
+        def _():
+            for copy in row_copies(there):
+                copy.wait_send()
+
     for copy in w_sends:
         copy.wait_send()
 
@@ -374,7 +399,7 @@
         vmem((ROWS, FEAT), BF16),
         vmem((ROWS, FEAT), BF16),
         vmem((ROWS, FEAT), BF16),
-        vmem((ROWS, HEADS), F32),
+        vmem((HEADS, ROWS), F32),
         vmem((ROWS, FEAT), BF16),
         vmem((HEADS, HD), F32),
         vmem((NX, FEAT, CW), BF16),
@@ -397,6 +422,7 @@
         vmem((NY, HD, HD), BF16),
         vmem((8, HD), F32),
         vmem((NY, 8, HD), F32),
+        vmem((HD, HD), F32),
         vmem((NZ, HD, HD), BF16),
         vmem((HEADS, HD, HD), BF16),
         vmem((NT, 2, HALF, CW), BF16),
@@ -420,7 +446,7 @@
     ]
     return pl.pallas_call(
         kernel,
-        out_shape=jax.ShapeDtypeStruct((ROWS, CW), BF16),
+        out_shape=pltpu.VMEM((ROWS, CW), BF16),
         in_specs=[pl.BlockSpec(memory_space=pl.ANY)] * 7,
         out_specs=pl.BlockSpec(memory_space=pltpu.VMEM),
         scratch_shapes=scratch,
@@ -432,7 +458,7 @@
             bytes_accessed=11_000_000,
             transcendentals=ROWS * FEAT * 4,
         ),
-    )(queries, keys, values, log_decay, gate, norm_gain.reshape(HEADS, HD), w_out)
+    )(queries, keys, values, log_decay.T, gate, norm_gain.reshape(HEADS, HD), w_out)
 
 
 def solution(mesh):

time: 53 us -> 45 us (0.85)
  the two profiles are of different devices: /device:TPU:1 before, /device:TPU:24 now
where the time goes in v2:
time: 45 us; the launch traced here: 44.3 us
  Pallas kernels  43.6 us (97%)
  local copies, waits for them, and re-layouts  0.75 us (2%)
    pallas_call x1, Pallas kernels, per_device(): pl.pallas_call(kernel, out_shape=pltpu.VMEM((ROWS, CW), BF16), in_specs=[...  43.6 us

profile of v2, /device:TPU:24, one launch (start us, length us, event | category | flops | bytes accessed | tf_op | source)
XLA Modules:
  0.0 44.3 jit_solution(9960343962182882007)
XLA Ops:
  0.0 43.6 %shard_map.73 = bf16[512,384]{1,0:T(8,128)(2,1)S(1)} custom-call(bf16[512,1024]{1,0:T(8,128)(2,1)} %q_hbm.1, bf16[512,1024]{1,0:T(8,128)(2,1)} %k_hbm.1, bf16[512,1024]{1,0:T(8,128)(2,1)} %v_hbm.1, f32[8,512]{1,0:T(8,128)} %bitcast.2, bf16[512,1024]{1,0:T(8,128)(2,1)} %gate_hbm.1, f32[8,128]{1,0:T(8,128)} %bitcast.3, bf16[1024,3072]{1,0:T(8,128)(2,1)} %w_hbm.1), custom_call_target="tpu_custom_call" | custom-call | flops 4026531840 | bytes 11000000 | tf_op jit(solution)/shard_map/pallas_call | solution.py:447
  43.6 0.7 %copy.9 = bf16[512,384]{1,0:T(8,128)(2,1)} copy(bf16[512,384]{1,0:T(8,128)(2,1)S(1)} %shard_map.73) | data formatting | bytes 786432

commit v3 on v2

--- a/solution.py
+++ b/solution.py
@@ -14,6 +14,9 @@
 CW = 384
 TILE = 128
 NT = ROWS // TILE
+PARTS = 2
+PD = HD // PARTS
+FAR_FIRST = (4, 5, 3, 6, 2, 7, 1)
 HALF = TILE // 2
 EARLY = 6
 
@@ -45,7 +48,7 @@
     lt, ltb, s_end, s_first, s_in, w_pre, cl_pre, t_out, t_in, rd_out, rd_in, rows_before, p_out, p_in,
     opp, side, held, fwd, mine, passing, fin,
     load_sem, lt_s, lt_r, s1, r1, t_s, t_r, rd_s, rd_r, s3, r3, w_s, w_r, h_s, h_r,
-    m1_s, m1_r, m2_s, m2_r, m3_s, m3_r,
+    m1_s, m1_r, m2_s, m2_r, m3_s, m3_r, ready_y, ready_x, ready_core,
 ):
     head, seq = lax.axis_index("head"), lax.axis_index("seq")
     z, y = lax.rem(seq, NZ), lax.div(seq, NZ)
@@ -61,11 +64,15 @@
     def along_y(off):
         return lax.rem(y + off, NY)
 
-    loads = [
-        pltpu.make_async_copy(src, dst, load_sem.at[i])
-        for i, (src, dst) in enumerate(
-            ((ld_hbm, ld), (k_hbm, k), (v_hbm, v), (q_hbm, q), (gate_hbm, gate), (gain_hbm, gain))
-        )
+    def load(i, src, dst):
+        return pltpu.make_async_copy(src, dst, load_sem.at[i])
+
+    ld_load = load(0, ld_hbm, ld)
+    kv_loads = [load(1, k_hbm, k), load(2, v_hbm, v)]
+    later_loads = [
+        load(3, q_hbm, q),
+        load(4, gate_hbm, gate),
+        load(5, gain_hbm, gain),
     ]
     w_loads = [
         pltpu.make_async_copy(
@@ -85,26 +92,45 @@
         )
         for i in range(NX)
     ]
-    for copy in loads:
+
+    barrier = pltpu.get_barrier_semaphore()
+
+    def greet(device):
+        pl.semaphore_signal(barrier, inc=1, device_id=device, device_id_type=MESH)
+
+    def answer(sem, device):
+        pl.semaphore_signal(sem, inc=1, device_id=device, device_id_type=MESH)
+
+    for off in FAR_FIRST:
+        greet({"seq": row0 + along_z(off)})
+    ld_load.start()
+    for copy in kv_loads:
         copy.start()
-
-    barrier = pltpu.get_barrier_semaphore()
-    for off in range(1, NZ):
-        pl.semaphore_signal(
-            barrier, inc=1, device_id={"seq": row0 + along_z(off)}, device_id_type=MESH
-        )
-    for off in range(1, NY):
-        pl.semaphore_signal(
-            barrier, inc=1, device_id={"seq": along_y(off) * NZ + z}, device_id_type=MESH
-        )
-    for device in (other, right, left):
-        pl.semaphore_signal(barrier, inc=1, device_id=device, device_id_type=MESH)
+    for there in range(1, NY):
+
+        @pl.when(there > y)
+        def _():
+            greet({"seq": there * NZ + z})
+
+    @pl.when(x_right > x)
+    def _():
+        greet(right)
+
+    @pl.when(x_left > x)
+    def _():
+        greet(left)
+
+    @pl.when(core == 0)
+    def _():
+        greet(other)
+
+    greeted = NZ - 1 + y + core + jnp.where(x_right < x, 1, 0) + jnp.where(x_left < x, 1, 0)
 
     at_row = lax.broadcasted_iota(jnp.int32, (BLOCK, BLOCK), 0)
     at_col = lax.broadcasted_iota(jnp.int32, (BLOCK, BLOCK), 1)
     lower = jnp.where(at_row >= at_col, 1.0, 0.0).astype(F32)
     upper = jnp.where(at_row <= at_col, 1.0, 0.0).astype(F32)
-    loads[0].wait()
+    ld_load.wait()
     for b in range(2):
         rows = slice(b * BLOCK, (b + 1) * BLOCK)
         decay = ld[:, rows]
@@ -124,53 +150,73 @@
             lt, ltb.at[z], lt_s.at[off], lt_r.at[z], {"seq": row0 + along_z(off)}
         )
 
-    def state_copy(h):
-        return remote(s_end.at[h], s_in.at[z], s1.at[h], r1.at[z], {"seq": row0 + h})
-
-    def make_state(h):
-        hc = columns(h)
-        parts = []
+    def state_copy(part, h):
+        return remote(
+            s_end.at[part, h],
+            s_in.at[part, z],
+            s1.at[part, h],
+            r1.at[part, z],
+            {"seq": row0 + h},
+        )
+
+    for copy in kv_loads:
+        copy.wait()
+    for h in range(HEADS):
+        hc = slice(h * HD, (h + 1) * HD)
+        ends = []
         for b in range(2):
             rows = slice(b * BLOCK, (b + 1) * BLOCK)
             total = cb[(b + 1) * BLOCK - 1 : (b + 1) * BLOCK, hc]
             weighted = (k[rows, hc].astype(F32) * jnp.exp(total - cb[rows, hc])).astype(BF16)
-            parts.append(
+            ends.append(
                 lax.dot_general(
                     weighted, v[rows, hc], (((0,), (0,)), ((), ())), preferred_element_type=F32
                 )
             )
-        s_first[h] = parts[0].astype(BF16)
-        s_end[h] = (jnp.exp(cb[ROWS - 1 : ROWS, hc]) * parts[0] + parts[1]).astype(BF16)
-
-    def far_first(i):
-        return along_z(4 + lax.div(i + 1, 2) * (2 * lax.rem(i, 2) - 1))
-
-    ready = jnp.where(z < NZ // 2, HEADS - 1, 1)
-    loads[1].wait()
-    loads[2].wait()
-
-    @pl.loop(0, HEADS)
-    def _(i):
-        make_state(far_first(i))
-
-        @pl.when(i == ready)
+        s_first[h] = ends[0].astype(BF16)
+        whole = (jnp.exp(cb[ROWS - 1 : ROWS, hc]) * ends[0] + ends[1]).astype(BF16)
+        for part in range(PARTS):
+            s_end[part, h] = whole[part * PD : (part + 1) * PD]
+
+    pl.semaphore_wait(barrier, greeted)
+    for part in range(PARTS):
+        for off in FAR_FIRST:
+            state_copy(part, along_z(off)).start()
+        if part == 0:
+            for off in FAR_FIRST:
+                lt_copy(off).start()
+    for part in range(PARTS):
+        s_in[part, z] = s_end[part, z]
+    for there in range(NY - 1):
+
+        @pl.when(there < y)
         def _():
-            pl.semaphore_wait(barrier, NZ - 1 + NY - 1 + 3)
-            for off in range(1, NZ):
-                lt_copy(off).start()
-
-        @pl.when(i >= ready)
-        def _():
-            @pl.loop(jnp.where(i == ready, 0, i), jnp.minimum(i + 1, HEADS - 1))
-            def _(j):
-                state_copy(far_first(j)).start()
-
-    s_in[z] = s_end[z]
+            answer(ready_y.at[y], {"seq": there * NZ + z})
+
+    @pl.when(x_right < x)
+    def _():
+        answer(ready_x.at[1], right)
+
+    @pl.when(x_left < x)
+    def _():
+        answer(ready_x.at[0], left)
+
+    @pl.when(core == 1)
+    def _():
+        answer(ready_core, other)
+
+    for copy in later_loads:
+        copy.start()
+
+    @pl.when(core == 0)
+    def _():
+        pl.semaphore_wait(ready_core, 1)
+
     for copy in w_sends:
         copy.start()
     for copy in w_loads:
         copy.start()
-    for copy in loads[3:]:
+    for copy in later_loads:
         copy.wait()
 
     def within(h):
@@ -201,64 +247,90 @@
     def _(h):
         within(h)
 
-    state = jnp.zeros((HD, HD), F32)
-    log = jnp.zeros((1, HD), F32)
-    for there in range(NZ):
-        w_pre[there] = state
-        cl_pre[there : there + 1, :] = log
+    def row_copy(part, there):
+        return remote(
+            t_out.at[part],
+            t_in.at[part, y],
+            t_s.at[part, there],
+            t_r.at[part, y],
+            {"seq": there * NZ + z},
+        )
+
+    def decay_copy(there):
+        return remote(
+            rd_out, rd_in.at[y], rd_s.at[there], rd_r.at[y], {"seq": there * NZ + z}
+        )
+
+    def prefix_copy(part, there):
+        return remote(
+            p_out.at[part, there],
+            p_in.at[part, z],
+            s3.at[part, there],
+            r3.at[part, z],
+            {"seq": row0 + there},
+        )
+
+    def prefix(part, there):
+        entering = jnp.exp(cl_pre[there : there + 1, :]) * rows_before[part] + w_pre[part, there]
+        p_out[part, there] = entering.astype(BF16)
 
         @pl.when(there != z)
         def _():
-            remote(lt, ltb.at[there], lt_s.at[0], lt_r.at[there], other).wait_recv()
-            remote(s_end.at[0], s_in.at[there], s1.at[0], r1.at[there], other).wait_recv()
-
-        step = ltb[there, pl.ds(z, 1), :]
-        state = jnp.exp(step) * state + s_in[there].astype(F32)
-        log = log + step
-    t_out[...] = state.astype(BF16)
-    rd_out[...] = jnp.broadcast_to(log, (8, HD))
-
-    def row_copies(there):
-        device = {"seq": there * NZ + z}
-        return (
-            remote(t_out, t_in.at[y], t_s.at[there], t_r.at[y], device),
-            remote(rd_out, rd_in.at[y], rd_s.at[there], rd_r.at[y], device),
-        )
-
-    for there in range(1, NY):
-
-        @pl.when(there > y)
-        def _():
-            for copy in row_copies(there):
-                copy.start()
-
-    rows_before[...] = jnp.zeros((HD, HD), F32)
-    for there in range(NY - 1):
-
-        @pl.when(there < y)
-        def _():
-            remote(t_out, t_in.at[there], t_s.at[0], t_r.at[there], other).wait_recv()
-            remote(rd_out, rd_in.at[there], rd_s.at[0], rd_r.at[there], other).wait_recv()
-            rows_before[...] = jnp.exp(rd_in[there][0:1, :]) * rows_before[...] + t_in[
-                there
-            ].astype(F32)
-
-    before = rows_before[...]
-
-    def prefix_copy(there):
-        return remote(
-            p_out.at[there], p_in.at[z], s3.at[there], r3.at[z], {"seq": row0 + there}
-        )
-
-    for there in range(NZ):
-        entering = (jnp.exp(cl_pre[there : there + 1, :]) * before + w_pre[there]).astype(BF16)
-        p_out[there] = entering
-
-        @pl.when(there != z)
-        def _():
-            prefix_copy(there).start()
-
-    p_in[z] = p_out[z]
+            prefix_copy(part, there).start()
+
+    for part in range(PARTS):
+        state = jnp.zeros((PD, HD), F32)
+        log = jnp.zeros((1, HD), F32)
+        for there in range(NZ):
+            w_pre[part, there] = state
+            if part == 0:
+                cl_pre[there : there + 1, :] = log
+
+            @pl.when(there != z)
+            def _():
+                if part == 0:
+                    remote(lt, ltb.at[there], lt_s.at[0], lt_r.at[there], other).wait_recv()
+                remote(
+                    s_end.at[part, 0], s_in.at[part, there], s1.at[0, 0], r1.at[part, there], other
+                ).wait_recv()
+
+            step = ltb[there, pl.ds(z, 1), :]
+            state = jnp.exp(step) * state + s_in[part, there].astype(F32)
+            log = log + step
+        t_out[part] = state.astype(BF16)
+        if part == 0:
+            rd_out[...] = jnp.broadcast_to(log, (8, HD))
+        for there in range(1, NY):
+
+            @pl.when(there > y)
+            def _():
+                if part == 0:
+                    pl.semaphore_wait(ready_y.at[there], 1)
+                    decay_copy(there).start()
+                row_copy(part, there).start()
+
+    for part in range(PARTS):
+        rows_before[part] = jnp.zeros((PD, HD), F32)
+        for there in range(NY - 1):
+
+            @pl.when(there < y)
+            def _():
+                if part == 0:
+                    remote(rd_out, rd_in.at[there], rd_s.at[0], rd_r.at[there], other).wait_recv()
+                remote(
+                    t_out.at[0], t_in.at[part, there], t_s.at[0, 0], t_r.at[part, there], other
+                ).wait_recv()
+                rows_before[part] = jnp.exp(rd_in[there][0:1, :]) * rows_before[part] + t_in[
+                    part, there
+                ].astype(F32)
+
+        for there in range(NZ // 2):
+            prefix(part, there)
+    for there in range(NZ // 2, NZ):
+        for part in range(PARTS):
+            prefix(part, there)
+    for part in range(PARTS):
+        p_in[part, z] = p_out[part, z]
 
     @pl.loop(EARLY, HEADS)
     def _(h):
@@ -270,7 +342,10 @@
         copy.wait_recv()
     for off in range(1, NZ):
         there = along_z(off)
-        remote(p_out.at[0], p_in.at[there], s3.at[0], r3.at[there], other).wait_recv()
+        for part in range(PARTS):
+            remote(
+                p_out.at[0, 0], p_in.at[part, there], s3.at[0, 0], r3.at[part, there], other
+            ).wait_recv()
 
     def tile(t):
         return pl.ds(pl.multiple_of(t * TILE, TILE), TILE)
@@ -282,8 +357,9 @@
         rows = tile(t)
         for h in range(HEADS):
             hc = slice(h * HD, (h + 1) * HD)
+            entering = jnp.concatenate([p_in[part, h] for part in range(PARTS)], axis=0)
             attended = att[rows, hc] + jnp.dot(
-                qs[rows, hc], p_in[h], preferred_element_type=F32
+                qs[rows, hc], entering, preferred_element_type=F32
             )
             square = jnp.mean(attended * attended, axis=1, keepdims=True)
             h_own[rows, hc] = (attended * lax.rsqrt(square + 1e-06) * gg[rows, hc]).astype(BF16)
@@ -332,6 +408,14 @@
             passing[way, t] = (held[way, t] + fwd[way, t].astype(F32)).astype(BF16)
             passing_copy(t, way).start()
 
+    @pl.when(x_right > x)
+    def _():
+        pl.semaphore_wait(ready_x.at[0], 1)
+
+    @pl.when(x_left > x)
+    def _():
+        pl.semaphore_wait(ready_x.at[1], 1)
+
     make_hidden(0)
 
     @pl.loop(0, NT)
@@ -350,11 +434,36 @@
         def _():
             pass_on(t - 1)
 
+    pass_on(NT - 1)
+
     @pl.loop(0, NT)
     def _(t):
         mine[t] = chunk(t, x)
 
-    pass_on(NT - 1)
+    for off in range(1, NZ):
+        lt_copy(off).wait_send()
+        there = along_z(off)
+        for part in range(PARTS):
+            state_copy(part, there).wait_send()
+            prefix_copy(part, there).wait_send()
+    for there in range(1, NY):
+
+        @pl.when(there > y)
+        def _():
+            decay_copy(there).wait_send()
+            for part in range(PARTS):
+                row_copy(part, there).wait_send()
+
+    for copy in w_sends:
+        copy.wait_send()
+
+    @pl.loop(0, NT)
+    def _(t):
+        hidden_copy(t).wait_send()
+        for way in range(2):
+            first_copy(t, way).wait_send()
+            side_copy(t, way).wait_send()
+            passing_copy(t, way).wait_send()
 
     @pl.loop(0, NT)
     def _(t):
@@ -369,29 +478,6 @@
                 + fin[1, t, half].astype(F32)
             ).astype(BF16)
 
-    for off in range(1, NZ):
-        lt_copy(off).wait_send()
-        there = along_z(off)
-        state_copy(there).wait_send()
-        prefix_copy(there).wait_send()
-    for there in range(1, NY):
-
-        @pl.when(there > y)
-        def _():
-            for copy in row_copies(there):
-                copy.wait_send()
-
-    for copy in w_sends:
-        copy.wait_send()
-
-    @pl.loop(0, NT)
-    def _(t):
-        hidden_copy(t).wait_send()
-        for way in range(2):
-            first_copy(t, way).wait_send()
-            side_copy(t, way).wait_send()
-            passing_copy(t, way).wait_send()
-
 
 def per_device(queries, keys, values, log_decay, gate, norm_gain, w_out):
     vmem, dma = pltpu.VMEM, pltpu.SemaphoreType.DMA
@@ -413,18 +499,18 @@
         vmem((ROWS, FEAT), BF16),
         vmem((HEADS, HD), F32),
         vmem((NZ, HEADS, HD), F32),
+        vmem((PARTS, HEADS, PD, HD), BF16),
         vmem((HEADS, HD, HD), BF16),
-        vmem((HEADS, HD, HD), BF16),
-        vmem((NZ, HD, HD), BF16),
-        vmem((NZ, HD, HD), F32),
+        vmem((PARTS, NZ, PD, HD), BF16),
+        vmem((PARTS, NZ, PD, HD), F32),
         vmem((NZ, HD), F32),
-        vmem((HD, HD), BF16),
-        vmem((NY, HD, HD), BF16),
+        vmem((PARTS, PD, HD), BF16),
+        vmem((PARTS, NY, PD, HD), BF16),
         vmem((8, HD), F32),
         vmem((NY, 8, HD), F32),
-        vmem((HD, HD), F32),
-        vmem((NZ, HD, HD), BF16),
-        vmem((HEADS, HD, HD), BF16),
+        vmem((PARTS, PD, HD), F32),
+        vmem((PARTS, NZ, PD, HD), BF16),
+        vmem((PARTS, HEADS, PD, HD), BF16),
         vmem((NT, 2, HALF, CW), BF16),
         vmem((2, NT, HALF, CW), BF16),
         vmem((2, NT, HALF, CW), F32),
@@ -434,15 +520,18 @@
         vmem((2, NT, 2, HALF, CW), BF16),
         dma((6 + NX,)),
         dma((NZ,)), dma((NZ,)),
-        dma((NZ,)), dma((NZ,)),
+        dma((PARTS, NZ)), dma((PARTS, NZ)),
+        dma((PARTS, NY)), dma((PARTS, NY)),
         dma((NY,)), dma((NY,)),
-        dma((NY,)), dma((NY,)),
-        dma((NZ,)), dma((NZ,)),
+        dma((PARTS, NZ)), dma((PARTS, NZ)),
         dma((NX,)), dma((NX,)),
         dma((NT,)), dma((NT,)),
         dma((2, NT)), dma((2, NT)),
         dma((2, NT)), dma((2, NT)),
         dma((2, NT)), dma((2, NT)),
+        pltpu.SemaphoreType.REGULAR((NY,)),
+        pltpu.SemaphoreType.REGULAR((2,)),
+        pltpu.SemaphoreType.REGULAR,
     ]
     return pl.pallas_call(
         kernel,

time: 45 us -> 44.6 us (level); the launches traced: 44.3 us -> 44.4 us
  no operation moved by 1% of the time
where the time goes in v3:
time: 44.6 us; the launch traced here: 44.4 us
  Pallas kernels  43.7 us (98%)
  local copies, waits for them, and re-layouts  0.75 us (2%)
    pallas_call x1, Pallas kernels, per_device(): pl.pallas_call(kernel, out_shape=pltpu.VMEM((ROWS, CW), BF16), in_specs=[...  43.7 us

profile of v3, /device:TPU:24, one launch (start us, length us, event | category | flops | bytes accessed | tf_op | source)
XLA Modules:
  0.0 44.4 jit_solution(14169044821851658016)
XLA Ops:
  0.0 43.7 %shard_map.73 = bf16[512,384]{1,0:T(8,128)(2,1)S(1)} custom-call(bf16[512,1024]{1,0:T(8,128)(2,1)} %q_hbm.1, bf16[512,1024]{1,0:T(8,128)(2,1)} %k_hbm.1, bf16[512,1024]{1,0:T(8,128)(2,1)} %v_hbm.1, f32[8,512]{1,0:T(8,128)} %bitcast.2, bf16[512,1024]{1,0:T(8,128)(2,1)} %gate_hbm.1, f32[8,128]{1,0:T(8,128)} %bitcast.3, bf16[1024,3072]{1,0:T(8,128)(2,1)} %w_hbm.1), custom_call_target="tpu_custom_call" | custom-call | flops 4026531840 | bytes 11000000 | tf_op jit(solution)/shard_map/pallas_call | solution.py:536
  43.7 0.7 %copy.9 = bf16[512,384]{1,0:T(8,128)(2,1)} copy(bf16[512,384]{1,0:T(8,128)(2,1)S(1)} %shard_map.73) | data formatting | bytes 786432

commit v4 on v3

--- a/solution.py
+++ b/solution.py
@@ -45,9 +45,9 @@
     out,
     q, k, v, ld, gate, gain, w_own, w_peer,
     cb, cumr, att, qs, gg, h_own, h_peer,
-    lt, ltb, s_end, s_first, s_in, w_pre, cl_pre, t_out, t_in, rd_out, rd_in, rows_before, p_out, p_in,
+    s_end, s_first, s_in, w_pre, cl_pre, t_out, t_in, rows_before, p_out, p_in,
     opp, side, held, fwd, mine, passing, fin,
-    load_sem, lt_s, lt_r, s1, r1, t_s, t_r, rd_s, rd_r, s3, r3, w_s, w_r, h_s, h_r,
+    load_sem, s1, r1, t_s, t_r, s3, r3, w_s, w_r, h_s, h_r,
     m1_s, m1_r, m2_s, m2_r, m3_s, m3_r, ready_y, ready_x, ready_core,
 ):
     head, seq = lax.axis_index("head"), lax.axis_index("seq")
@@ -140,20 +140,30 @@
         cumr[:, rows] = jnp.dot(decay, upper, precision=EXACT, preferred_element_type=F32)
         for h in range(HEADS):
             cb[rows, h * HD : (h + 1) * HD] = jnp.broadcast_to(cum[:, h : h + 1], (BLOCK, HD))
-    lt[...] = jnp.broadcast_to(
-        cumr[:, BLOCK - 1 : BLOCK] + cumr[:, ROWS - 1 : ROWS], (HEADS, HD)
-    )
-    ltb[z] = lt[...]
-
-    def lt_copy(off):
-        return remote(
-            lt, ltb.at[z], lt_s.at[off], lt_r.at[z], {"seq": row0 + along_z(off)}
-        )
+
+    def rows_of(part):
+        return PD + 16 if part == 0 else PD
+
+    row_at = lax.broadcasted_iota(jnp.int32, (16, HD), 0)
+
+    def split_rows(log):
+        high = log.astype(BF16).astype(F32)
+        middle = (log - high).astype(BF16).astype(F32)
+        low = log - high - middle
+        return jnp.where(
+            row_at == 0,
+            high,
+            jnp.where(row_at == 1, middle, jnp.where(row_at == 2, low, 0.0)),
+        ).astype(BF16)
+
+    def joined_rows(split):
+        wide = split.astype(F32)
+        return wide[0:1] + wide[1:2] + wide[2:3]
 
     def state_copy(part, h):
         return remote(
-            s_end.at[part, h],
-            s_in.at[part, z],
+            s_end.at[part, h, 0 : rows_of(part)],
+            s_in.at[part, z, 0 : rows_of(part)],
             s1.at[part, h],
             r1.at[part, z],
             {"seq": row0 + h},
@@ -176,15 +186,13 @@
         s_first[h] = ends[0].astype(BF16)
         whole = (jnp.exp(cb[ROWS - 1 : ROWS, hc]) * ends[0] + ends[1]).astype(BF16)
         for part in range(PARTS):
-            s_end[part, h] = whole[part * PD : (part + 1) * PD]
+            s_end[part, h, 0:PD] = whole[part * PD : (part + 1) * PD]
+        s_end[0, h, PD : PD + 16] = split_rows(cb[BLOCK - 1 : BLOCK, hc] + cb[ROWS - 1 : ROWS, hc])
 
     pl.semaphore_wait(barrier, greeted)
     for part in range(PARTS):
         for off in FAR_FIRST:
             state_copy(part, along_z(off)).start()
-        if part == 0:
-            for off in FAR_FIRST:
-                lt_copy(off).start()
     for part in range(PARTS):
         s_in[part, z] = s_end[part, z]
     for there in range(NY - 1):
@@ -249,16 +257,11 @@
 
     def row_copy(part, there):
         return remote(
-            t_out.at[part],
-            t_in.at[part, y],
+            t_out.at[part, 0 : rows_of(part)],
+            t_in.at[part, y, 0 : rows_of(part)],
             t_s.at[part, there],
             t_r.at[part, y],
             {"seq": there * NZ + z},
-        )
-
-    def decay_copy(there):
-        return remote(
-            rd_out, rd_in.at[y], rd_s.at[there], rd_r.at[y], {"seq": there * NZ + z}
         )
 
     def prefix_copy(part, there):
@@ -288,25 +291,26 @@
 
             @pl.when(there != z)
             def _():
-                if part == 0:
-                    remote(lt, ltb.at[there], lt_s.at[0], lt_r.at[there], other).wait_recv()
                 remote(
-                    s_end.at[part, 0], s_in.at[part, there], s1.at[0, 0], r1.at[part, there], other
+                    s_end.at[part, 0, 0 : rows_of(part)],
+                    s_in.at[part, there, 0 : rows_of(part)],
+                    s1.at[0, 0],
+                    r1.at[part, there],
+                    other,
                 ).wait_recv()
 
-            step = ltb[there, pl.ds(z, 1), :]
-            state = jnp.exp(step) * state + s_in[part, there].astype(F32)
+            step = joined_rows(s_in[0, there, PD : PD + 16])
+            state = jnp.exp(step) * state + s_in[part, there, 0:PD].astype(F32)
             log = log + step
-        t_out[part] = state.astype(BF16)
+        t_out[part, 0:PD] = state.astype(BF16)
         if part == 0:
-            rd_out[...] = jnp.broadcast_to(log, (8, HD))
+            t_out[0, PD : PD + 16] = split_rows(log)
         for there in range(1, NY):
 
             @pl.when(there > y)
             def _():
                 if part == 0:
                     pl.semaphore_wait(ready_y.at[there], 1)
-                    decay_copy(there).start()
                 row_copy(part, there).start()
 
     for part in range(PARTS):
@@ -315,14 +319,16 @@
 
             @pl.when(there < y)
             def _():
-                if part == 0:
-                    remote(rd_out, rd_in.at[there], rd_s.at[0], rd_r.at[there], other).wait_recv()
                 remote(
-                    t_out.at[0], t_in.at[part, there], t_s.at[0, 0], t_r.at[part, there], other
+                    t_out.at[part, 0 : rows_of(part)],
+                    t_in.at[part, there, 0 : rows_of(part)],
+                    t_s.at[0, 0],
+                    t_r.at[part, there],
+                    other,
                 ).wait_recv()
-                rows_before[part] = jnp.exp(rd_in[there][0:1, :]) * rows_before[part] + t_in[
-                    part, there
-                ].astype(F32)
+                rows_before[part] = jnp.exp(
+                    joined_rows(t_in[0, there, PD : PD + 16])
+                ) * rows_before[part] + t_in[part, there, 0:PD].astype(F32)
 
         for there in range(NZ // 2):
             prefix(part, there)
@@ -441,7 +447,6 @@
         mine[t] = chunk(t, x)
 
     for off in range(1, NZ):
-        lt_copy(off).wait_send()
         there = along_z(off)
         for part in range(PARTS):
             state_copy(part, there).wait_send()
@@ -450,7 +455,6 @@
 
         @pl.when(there > y)
         def _():
-            decay_copy(there).wait_send()
             for part in range(PARTS):
                 row_copy(part, there).wait_send()
 
@@ -497,17 +501,13 @@
         vmem((ROWS, FEAT), F32),
         vmem((ROWS, FEAT), BF16),
         vmem((ROWS, FEAT), BF16),
-        vmem((HEADS, HD), F32),
-        vmem((NZ, HEADS, HD), F32),
-        vmem((PARTS, HEADS, PD, HD), BF16),
+        vmem((PARTS, HEADS, PD + 16, HD), BF16),
         vmem((HEADS, HD, HD), BF16),
-        vmem((PARTS, NZ, PD, HD), BF16),
+        vmem((PARTS, NZ, PD + 16, HD), BF16),
         vmem((PARTS, NZ, PD, HD), F32),
         vmem((NZ, HD), F32),
-        vmem((PARTS, PD, HD), BF16),
-        vmem((PARTS, NY, PD, HD), BF16),
-        vmem((8, HD), F32),
-        vmem((NY, 8, HD), F32),
+        vmem((PARTS, PD + 16, HD), BF16),
+        vmem((PARTS, NY, PD + 16, HD), BF16),
         vmem((PARTS, PD, HD), F32),
         vmem((PARTS, NZ, PD, HD), BF16),
         vmem((PARTS, HEADS, PD, HD), BF16),
@@ -519,10 +519,8 @@
         vmem((2, NT, HALF, CW), BF16),
         vmem((2, NT, 2, HALF, CW), BF16),
         dma((6 + NX,)),
-        dma((NZ,)), dma((NZ,)),
         dma((PARTS, NZ)), dma((PARTS, NZ)),
         dma((PARTS, NY)), dma((PARTS, NY)),
-        dma((NY,)), dma((NY,)),
         dma((PARTS, NZ)), dma((PARTS, NZ)),
         dma((NX,)), dma((NX,)),
         dma((NT,)), dma((NT,)),

time: 44.6 us -> 44.3 us (level)
  no operation moved by 1% of the time
where the time goes in v4:
time: 44.3 us; the launch traced here: 44.2 us
  Pallas kernels  43.4 us (98%)
  local copies, waits for them, and re-layouts  0.75 us (2%)
    pallas_call x1, Pallas kernels, per_device(): pl.pallas_call(kernel, out_shape=pltpu.VMEM((ROWS, CW), BF16), in_specs=[...  43.4 us

profile of v4, /device:TPU:24, one launch (start us, length us, event | category | flops | bytes accessed | tf_op | source)
XLA Modules:
  0.0 44.2 jit_solution(15109758148115088822)
XLA Ops:
  0.0 43.4 %shard_map.73 = bf16[512,384]{1,0:T(8,128)(2,1)S(1)} custom-call(bf16[512,1024]{1,0:T(8,128)(2,1)} %q_hbm.1, bf16[512,1024]{1,0:T(8,128)(2,1)} %k_hbm.1, bf16[512,1024]{1,0:T(8,128)(2,1)} %v_hbm.1, f32[8,512]{1,0:T(8,128)} %bitcast.2, bf16[512,1024]{1,0:T(8,128)(2,1)} %gate_hbm.1, f32[8,128]{1,0:T(8,128)} %bitcast.3, bf16[1024,3072]{1,0:T(8,128)(2,1)} %w_hbm.1), custom_call_target="tpu_custom_call" | custom-call | flops 4026531840 | bytes 11000000 | tf_op jit(solution)/shard_map/pallas_call | solution.py:534
  43.4 0.7 %copy.9 = bf16[512,384]{1,0:T(8,128)(2,1)} copy(bf16[512,384]{1,0:T(8,128)(2,1)S(1)} %shard_map.73) | data formatting | bytes 786432

commit v5 on v4

--- a/solution.py
+++ b/solution.py
@@ -18,7 +18,7 @@
 PD = HD // PARTS
 FAR_FIRST = (4, 5, 3, 6, 2, 7, 1)
 HALF = TILE // 2
-EARLY = 6
+EARLY = 8
 
 F32, BF16 = jnp.float32, jnp.bfloat16
 EXACT = lax.Precision.HIGHEST
@@ -273,10 +273,11 @@
             {"seq": row0 + there},
         )
 
-    def prefix(part, there):
+    def enter(part, there):
         entering = jnp.exp(cl_pre[there : there + 1, :]) * rows_before[part] + w_pre[part, there]
         p_out[part, there] = entering.astype(BF16)
 
+    def send_prefix(part, there):
         @pl.when(there != z)
         def _():
             prefix_copy(part, there).start()
@@ -284,24 +285,26 @@
     for part in range(PARTS):
         state = jnp.zeros((PD, HD), F32)
         log = jnp.zeros((1, HD), F32)
-        for there in range(NZ):
-            w_pre[part, there] = state
-            if part == 0:
-                cl_pre[there : there + 1, :] = log
-
-            @pl.when(there != z)
-            def _():
-                remote(
-                    s_end.at[part, 0, 0 : rows_of(part)],
-                    s_in.at[part, there, 0 : rows_of(part)],
-                    s1.at[0, 0],
-                    r1.at[part, there],
-                    other,
-                ).wait_recv()
-
-            step = joined_rows(s_in[0, there, PD : PD + 16])
-            state = jnp.exp(step) * state + s_in[part, there, 0:PD].astype(F32)
-            log = log + step
+        for first in range(0, NZ, NZ // 2):
+            for there in range(first, first + NZ // 2):
+
+                @pl.when(there != z)
+                def _():
+                    remote(
+                        s_end.at[part, 0, 0 : rows_of(part)],
+                        s_in.at[part, there, 0 : rows_of(part)],
+                        s1.at[0, 0],
+                        r1.at[part, there],
+                        other,
+                    ).wait_recv()
+
+            for there in range(first, first + NZ // 2):
+                w_pre[part, there] = state
+                if part == 0:
+                    cl_pre[there : there + 1, :] = log
+                step = joined_rows(s_in[0, there, PD : PD + 16])
+                state = jnp.exp(step) * state + s_in[part, there, 0:PD].astype(F32)
+                log = log + step
         t_out[part, 0:PD] = state.astype(BF16)
         if part == 0:
             t_out[0, PD : PD + 16] = split_rows(log)
@@ -331,10 +334,14 @@
                 ) * rows_before[part] + t_in[part, there, 0:PD].astype(F32)
 
         for there in range(NZ // 2):
-            prefix(part, there)
-    for there in range(NZ // 2, NZ):
-        for part in range(PARTS):
-            prefix(part, there)
+            enter(part, there)
+        for there in range(NZ // 2):
+            send_prefix(part, there)
+    for part in range(PARTS):
+        for there in range(NZ // 2, NZ):
+            enter(part, there)
+        for there in range(NZ // 2, NZ):
+            send_prefix(part, there)
     for part in range(PARTS):
         p_in[part, z] = p_out[part, z]
 
@@ -372,8 +379,11 @@
         hidden_copy(t).start()
 
     def chunk(t, i):
-        return jnp.dot(h_own[tile(t), :], w_own[i], preferred_element_type=F32) + jnp.dot(
-            h_peer[tile(t), :], w_peer[i], preferred_element_type=F32
+        hidden = jnp.concatenate([h_own[tile(t), :], h_peer[tile(t), :]], axis=1)
+        return jnp.dot(
+            hidden,
+            jnp.concatenate([w_own[i], w_peer[i]], axis=0),
+            preferred_element_type=F32,
         )
 
     targets = (right, left)
@@ -402,7 +412,7 @@
             first_copy(t, way).start()
 
     def send_near(t):
-        for way, i in enumerate((x_right, x_left)):
+        for way, i in ((1, x_left), (0, x_right)):
             near = chunk(t, i)
             side[way, t] = near[halves[1 - way]].astype(BF16)
             side_copy(t, way).start()

time: 44.3 us -> 44.2 us (level)
  no operation moved by 1% of the time
where the time goes in v5:
time: 44.2 us; the launch traced here: 44 us
  Pallas kernels  43.3 us (98%)
  local copies, waits for them, and re-layouts  0.75 us (2%)
    pallas_call x1, Pallas kernels, per_device(): pl.pallas_call(kernel, out_shape=pltpu.VMEM((ROWS, CW), BF16), in_specs=[...  43.3 us

profile of v5, /device:TPU:24, one launch (start us, length us, event | category | flops | bytes accessed | tf_op | source)
XLA Modules:
  0.0 44.0 jit_solution(248841453344248410)
XLA Ops:
  0.0 43.3 %shard_map.73 = bf16[512,384]{1,0:T(8,128)(2,1)S(1)} custom-call(bf16[512,1024]{1,0:T(8,128)(2,1)} %q_hbm.1, bf16[512,1024]{1,0:T(8,128)(2,1)} %k_hbm.1, bf16[512,1024]{1,0:T(8,128)(2,1)} %v_hbm.1, f32[8,512]{1,0:T(8,128)} %bitcast.2, bf16[512,1024]{1,0:T(8,128)(2,1)} %gate_hbm.1, f32[8,128]{1,0:T(8,128)} %bitcast.3, bf16[1024,3072]{1,0:T(8,128)(2,1)} %w_hbm.1), custom_call_target="tpu_custom_call" | custom-call | flops 4026531840 | bytes 11000000 | tf_op jit(solution)/shard_map/pallas_call | solution.py:544
  43.3 0.7 %copy.9 = bf16[512,384]{1,0:T(8,128)(2,1)} copy(bf16[512,384]{1,0:T(8,128)(2,1)S(1)} %shard_map.73) | data formatting | bytes 786432

commit v6 on v4

--- a/solution.py
+++ b/solution.py
@@ -18,7 +18,7 @@
 PD = HD // PARTS
 FAR_FIRST = (4, 5, 3, 6, 2, 7, 1)
 HALF = TILE // 2
-EARLY = 6
+EARLY = 8
 
 F32, BF16 = jnp.float32, jnp.bfloat16
 EXACT = lax.Precision.HIGHEST
@@ -402,7 +402,7 @@
             first_copy(t, way).start()
 
     def send_near(t):
-        for way, i in enumerate((x_right, x_left)):
+        for way, i in ((1, x_left), (0, x_right)):
             near = chunk(t, i)
             side[way, t] = near[halves[1 - way]].astype(BF16)
             side_copy(t, way).start()

time: 44.3 us -> 44.2 us (level)
  no operation moved by 1% of the time
where the time goes in v6:
time: 44.2 us; the launch traced here: 44 us
  Pallas kernels  43.3 us (98%)
  local copies, waits for them, and re-layouts  0.75 us (2%)
    pallas_call x1, Pallas kernels, per_device(): pl.pallas_call(kernel, out_shape=pltpu.VMEM((ROWS, CW), BF16), in_specs=[...  43.3 us

profile of v6, /device:TPU:24, one launch (start us, length us, event | category | flops | bytes accessed | tf_op | source)
XLA Modules:
  0.0 44.0 jit_solution(2162543723311550647)
XLA Ops:
  0.0 43.3 %shard_map.73 = bf16[512,384]{1,0:T(8,128)(2,1)S(1)} custom-call(bf16[512,1024]{1,0:T(8,128)(2,1)} %q_hbm.1, bf16[512,1024]{1,0:T(8,128)(2,1)} %k_hbm.1, bf16[512,1024]{1,0:T(8,128)(2,1)} %v_hbm.1, f32[8,512]{1,0:T(8,128)} %bitcast.2, bf16[512,1024]{1,0:T(8,128)(2,1)} %gate_hbm.1, f32[8,128]{1,0:T(8,128)} %bitcast.3, bf16[1024,3072]{1,0:T(8,128)(2,1)} %w_hbm.1), custom_call_target="tpu_custom_call" | custom-call | flops 4026531840 | bytes 11000000 | tf_op jit(solution)/shard_map/pallas_call | solution.py:534
  43.3 0.7 %copy.9 = bf16[512,384]{1,0:T(8,128)(2,1)} copy(bf16[512,384]{1,0:T(8,128)(2,1)S(1)} %shard_map.73) | data formatting | bytes 786432
